TPU v7x, 512 devices: a whole 4x8x8 slice. The times are simulated.
512 devices in a mesh: tile: 128 (over z, y, core), cam: 4 (over x).
Axes of the slice: x: 4, y: 8, z: 8, core: 2. Of those that a mesh axis runs over, the one named last changes fastest.
Arguments:
- gaussians: float32 [59, 65536], P(None, 'tile')
- moment_one: float32 [59, 65536], P(None, 'tile'), may hold values from -3 to 3
- moment_two: float32 [59, 65536], P(None, 'tile'), may hold values from 0.01 to 1
- cameras: float32 [4, 4], P('cam')
- requests: int32 [4, 131072], P('cam', 'tile'), may hold values from 0 to 511
- tile_lists: int32 [4, 128, 1024], P('cam', 'tile'), may hold values from 0 to 1023
- tile_lengths: int32 [4, 128], P('cam', 'tile'), may hold values from 1 to 1024, as said below
- cotangent: float32 [4, 128, 3, 256], P('cam', 'tile'), may hold values from -6 to 6
Outputs:
- gradient: float32 [59, 65536], P(None, 'tile')
- updated: float32 [59, 65536], P(None, 'tile')
- first_new: float32 [59, 65536], P(None, 'tile')
- second_new: float32 [59, 65536], P(None, 'tile')
Inputs may be any that keep to these rules, and one draw needn't show every extreme that they name: `requests`: each device asks every owner, for each camera, for exactly 8 rows by local index; a row may be asked more than once. `tile_lists`: slot o * 8 + s names the s-th row fetched from owner o by the device holding the tile. `tile_lengths`: slots from the length on are unused; some tile of every draw is full.
All inputs are finite; a program needn't handle non-finite values.
Results may differ from a plain program's by a relative error of at most 0.0003.
Values sent between devices are 32-bit elements; how exact they have to be, the bound alone decides.
A program may use at most 64 MiB of HBM per device.

v0:
```python
import jax
import jax.numpy as jnp
from jax import lax
from jax.experimental import pallas as pl
from jax.experimental.pallas import tpu as pltpu
from jax.sharding import PartitionSpec as P

f32 = jnp.float32
bf16 = jnp.bfloat16
MESH = pl.DeviceIdType.MESH
N_TILE = 128
N_CAM = 4
OWN = 512
SLOTS = 1024
PIX = 256
GROUP = 256
SHIFT = 32

focal_length = 350.0
dilation = 0.3
sh_zero = 0.28209479177387814
sh_one = 0.4886025119029199
sh_two = [
    1.0925484305920792,
    -1.0925484305920792,
    0.31539156525252005,
    -1.0925484305920792,
    0.5462742152960396,
]
sh_three = [
    -0.5900435899266435,
    2.890611442640554,
    -0.4570457994644658,
    0.3731763325901154,
    -0.4570457994644658,
    1.445305721320277,
    -0.5900435899266435,
]


def harmonics(dir_x, dir_y, dir_z):
    xx = dir_x * dir_x
    yy = dir_y * dir_y
    zz = dir_z * dir_z
    return [
        jnp.full_like(dir_x, sh_zero),
        -sh_one * dir_y,
        sh_one * dir_z,
        -sh_one * dir_x,
        sh_two[0] * dir_x * dir_y,
        sh_two[1] * dir_y * dir_z,
        sh_two[2] * (2.0 * zz - xx - yy),
        sh_two[3] * dir_x * dir_z,
        sh_two[4] * (xx - yy),
        sh_three[0] * dir_y * (3.0 * xx - yy),
        sh_three[1] * dir_x * dir_y * dir_z,
        sh_three[2] * dir_y * (4.0 * zz - xx - yy),
        sh_three[3] * dir_z * (2.0 * zz - 3.0 * xx - 3.0 * yy),
        sh_three[4] * dir_x * (4.0 * zz - xx - yy),
        sh_three[5] * dir_z * (xx - yy),
        sh_three[6] * dir_x * (xx - 3.0 * yy),
    ]


def screen_of(rows, camera, cos_yaw, sin_yaw):
    rel_x = rows[0] - camera[0]
    rel_y = rows[1] - camera[1]
    rel_z = rows[2] - camera[2]
    cam_x = cos_yaw * rel_x - sin_yaw * rel_z
    cam_z = sin_yaw * rel_x + cos_yaw * rel_z
    inv_depth = 1.0 / cam_z
    scaled = focal_length * inv_depth
    screen_x = scaled * cam_x + 128.0
    screen_y = scaled * rel_y + 64.0
    slant_x = -scaled * cam_x * inv_depth
    slant_y = -scaled * rel_y * inv_depth
    proj = [
        [scaled * cos_yaw + slant_x * sin_yaw, None, slant_x * cos_yaw - scaled * sin_yaw],
        [slant_y * sin_yaw, scaled, slant_y * cos_yaw],
    ]
    quat_norm = jnp.sqrt(
        rows[6] * rows[6] + rows[7] * rows[7] + rows[8] * rows[8] + rows[9] * rows[9]
    )
    inv_norm = 1.0 / quat_norm
    quat_w = rows[6] * inv_norm
    quat_x = rows[7] * inv_norm
    quat_y = rows[8] * inv_norm
    quat_z = rows[9] * inv_norm
    rotation = [
        [
            1.0 - 2.0 * (quat_y * quat_y + quat_z * quat_z),
            2.0 * (quat_x * quat_y - quat_w * quat_z),
            2.0 * (quat_x * quat_z + quat_w * quat_y),
        ],
        [
            2.0 * (quat_x * quat_y + quat_w * quat_z),
            1.0 - 2.0 * (quat_x * quat_x + quat_z * quat_z),
            2.0 * (quat_y * quat_z - quat_w * quat_x),
        ],
        [
            2.0 * (quat_x * quat_z - quat_w * quat_y),
            2.0 * (quat_y * quat_z + quat_w * quat_x),
            1.0 - 2.0 * (quat_x * quat_x + quat_y * quat_y),
        ],
    ]
    scales = [jnp.exp(rows[3]), jnp.exp(rows[4]), jnp.exp(rows[5])]
    shape_of = [[rotation[i][j] * scales[j] for j in range(3)] for i in range(3)]
    spread = [
        [proj[0][0] * shape_of[0][j] + proj[0][2] * shape_of[2][j] for j in range(3)],
        [
            proj[1][0] * shape_of[0][j] + proj[1][1] * shape_of[1][j] + proj[1][2] * shape_of[2][j]
            for j in range(3)
        ],
    ]
    cov_a = spread[0][0] ** 2 + spread[0][1] ** 2 + spread[0][2] ** 2 + dilation
    cov_b = spread[0][0] * spread[1][0] + spread[0][1] * spread[1][1] + spread[0][2] * spread[1][2]
    cov_c = spread[1][0] ** 2 + spread[1][1] ** 2 + spread[1][2] ** 2 + dilation
    inv_det = 1.0 / (cov_a * cov_c - cov_b * cov_b)
    inv_dist = 1.0 / jnp.sqrt(rel_x * rel_x + rel_y * rel_y + rel_z * rel_z)
    basis = harmonics(rel_x * inv_dist, rel_y * inv_dist, rel_z * inv_dist)
    colours = []
    for channel in range(3):
        acc_col = 0.5 + basis[0] * rows[11 + 16 * channel]
        for order in range(1, 16):
            acc_col = acc_col + basis[order] * rows[11 + 16 * channel + order]
        colours.append(acc_col)
    return [screen_x, screen_y, cov_c * inv_det, -cov_b * inv_det, cov_a * inv_det, *colours]


def parts_of(value, count):
    out = []
    for _ in range(count):
        part = value.astype(bf16).astype(f32)
        out.append(part)
        value = value - part
    return out


def dot(left, right, dims=((1,), (0,))):
    return lax.dot_general(left, right, (dims, ((), ())), preferred_element_type=f32)


def stack_rows(rows, count):
    width = rows[0].shape[1]
    at = lax.broadcasted_iota(jnp.int32, (count, width), 0)
    out = jnp.zeros((count, width), f32)
    for i, row in enumerate(rows):
        out = jnp.where(at == i, row, out)
    return out


def wait_for(ref, sem):
    pltpu.make_async_copy(ref, ref, sem).wait()


def splat_kernel(
    gauss_ref, camera_ref, req_ref, list_ref, length_ref, cot_ref,
    out_ref,
    ask_out, ask_in, row_out, row_in, grad_out, grad_in, cam_out,
    picked, at_owner, expo, gain, alpha, keep_a, keep_b, before, weight_a, weight_b,
    drop_a, drop_b, behind, wgain, turned,
    *sems,
):
    me = lax.axis_index("tile")
    cam = lax.axis_index("cam")
    high = me // 16
    low = lax.rem(me, 16)

    barrier = pltpu.get_barrier_semaphore()

    @pl.loop(1, N_TILE)
    def _(i):
        pl.semaphore_signal(
            barrier, inc=1, device_id=(lax.rem(me + i, N_TILE), cam), device_id_type=MESH
        )

    for i in range(1, N_CAM):
        pl.semaphore_signal(
            barrier, inc=1, device_id=(me, lax.rem(cam + i, N_CAM)), device_id_type=MESH
        )

    def exchange(src, dst, send_sem, recv_sem, source_of):
        @pl.loop(1, N_TILE)
        def _(i):
            peer = lax.rem(me + i, N_TILE)
            pltpu.make_async_remote_copy(
                src.at[source_of(peer)], dst.at[me], send_sem, recv_sem,
                device_id=(peer, cam), device_id_type=MESH,
            ).start()

    for z in range(8):
        ask_out[z] = req_ref[:, 128 * z : 128 * (z + 1)]
    camera = camera_ref[...]
    heading = camera[:, 3:4]
    cos_yaw = jnp.cos(heading)
    sin_yaw = jnp.sin(heading)
    rows = [gauss_ref[i : i + 1, :] for i in range(59)]
    values = screen_of(
        rows, [camera[:, 0:1], camera[:, 1:2], camera[:, 2:3]], cos_yaw, sin_yaw
    )
    opacity = 1.0 / (1.0 + jnp.exp(-rows[10]))
    zero = jnp.zeros_like(opacity)
    table = stack_rows([*values[:5], opacity, zero, zero, *values[5:]], 16)
    table = jnp.concatenate(parts_of(table, 3), axis=0).astype(bf16)
    cam_rows = stack_rows(
        [jnp.broadcast_to(v, (1, OWN)) for v in
         (camera[:, 0:1], camera[:, 1:2], camera[:, 2:3], cos_yaw, sin_yaw)],
        8,
    )

    pl.semaphore_wait(barrier, N_TILE - 1 + N_CAM - 1)
    exchange(ask_out, ask_in, sems[0], sems[1], lambda peer: peer // 16)
    ask_in[me] = ask_out[high]

    list_row = list_ref[0]
    slot_owner = lax.shift_right_logical(list_row, 3)
    slot_part = jnp.bitwise_and(list_row, 7)
    at_owner[...] = jnp.where(
        lax.broadcasted_iota(jnp.int32, (N_TILE, SLOTS), 0) == slot_owner, 1.0, 0.0
    ).astype(bf16)
    live = (
        lax.broadcasted_iota(jnp.int32, (1, SLOTS), 1) < jnp.broadcast_to(length_ref[...], (1, SLOTS))
    )
    pixel = lax.broadcasted_iota(jnp.int32, (1, PIX), 1)
    loc_x = jnp.bitwise_and(pixel, 15).astype(f32) - 7.5
    loc_y = lax.shift_right_logical(pixel, 4).astype(f32) - 7.5
    basis = stack_rows(
        [loc_x * loc_x, loc_y * loc_y, loc_x * loc_y, loc_x, loc_y, jnp.ones_like(loc_x)], 8
    )
    cot = jnp.concatenate([cot_ref[0, 0], jnp.zeros((5, PIX), f32)], axis=0)
    cot_h, cot_m, cot_l = parts_of(cot, 3)
    wide = jnp.concatenate(
        [basis, basis, basis, cot_h, cot_h, cot_h, cot_m, cot_m, cot_l, jnp.zeros((56, PIX), f32)],
        axis=0,
    )
    wide = jnp.transpose(wide).astype(bf16)
    basis_cols = wide[:, 0:24]
    cot_cols = wide[:, 24:72]
    cot_rows = jnp.concatenate([cot_h, cot_m], axis=0).astype(bf16)
    basis_rows = jnp.concatenate([basis, jnp.zeros_like(basis)], axis=0).astype(bf16)
    up = lax.broadcasted_iota(jnp.int32, (GROUP, GROUP), 0)
    down = lax.broadcasted_iota(jnp.int32, (GROUP, GROUP), 1)
    earlier = jnp.where(up < down, 1.0, 0.0).astype(bf16)
    later = jnp.where(up > down, 1.0, 0.0).astype(bf16)
    ones = jnp.ones((GROUP, 128), bf16)

    wait_for(ask_in.at[pl.ds(0, N_TILE - 1)], sems[1])

    asked = jnp.transpose(ask_in[:, 0, :])
    turned[...] = asked
    asked = turned[pl.ds(pl.multiple_of(low * 8, 8), 8), :]
    own_at = lax.broadcasted_iota(jnp.int32, (OWN, 128), 0)
    for s in range(8):
        picked[:, 128 * s : 128 * (s + 1)] = jnp.where(
            own_at == asked[s : s + 1, :], 1.0, 0.0
        ).astype(bf16)
    found = dot(table, picked[...])
    found = found[0:16] + found[16:32] + found[32:48]
    found = jnp.concatenate([found[:, 128 * s : 128 * (s + 1)] for s in range(8)], axis=0)
    row_out[:, 0, :] = jnp.transpose(found)
    exchange(row_out, row_in, sems[2], sems[3], lambda peer: peer)
    row_in[me] = row_out[me]
    wait_for(row_in.at[pl.ds(0, N_TILE - 1)], sems[3])

    got = jnp.transpose(row_in[:, 0, :])
    got = jnp.concatenate(parts_of(got, 3), axis=0).astype(bf16)
    listed = dot(got, at_owner[...])
    listed = listed[0:128] + listed[128:256] + listed[256:384]
    slot = jnp.zeros((16, SLOTS), f32)
    for s in range(8):
        slot = slot + jnp.where(slot_part == s, listed[16 * s : 16 * (s + 1)], 0.0)
    tile_x = (lax.rem(me, 16) * 16 + 8).astype(f32)
    tile_y = (high * 16 + 8).astype(f32)
    off_x = slot[0:1] - tile_x
    off_y = slot[1:2] - tile_y
    con_a, con_b, con_c = slot[2:3], slot[3:4], slot[4:5]
    op_live = jnp.where(live, slot[5:6], 0.0)
    push_x = con_a * off_x + con_b * off_y
    push_y = con_c * off_y + con_b * off_x
    coef = stack_rows(
        [-0.5 * con_a, -0.5 * con_c, -con_b, push_x, push_y,
         -0.5 * (off_x * push_x + off_y * push_y)],
        8,
    )
    coef = jnp.concatenate(parts_of(coef, 3), axis=0).astype(bf16)
    colour = parts_of(slot[8:16], 3)
    colour = jnp.concatenate(
        [colour[0], colour[1], colour[2], colour[0], colour[1], colour[0]], axis=0
    ).astype(bf16)
    expo[...] = dot(basis_cols, coef)
    gain[...] = dot(cot_cols, colour)

    groups = range(SLOTS // GROUP)

    def blocks(group, step):
        cols = slice(GROUP * group, GROUP * (group + 1))

        @pl.loop(0, PIX // SHIFT)
        def _(i):
            step((pl.ds(pl.multiple_of(i * SHIFT, SHIFT), SHIFT), cols))

    def split_to(value, ref_a, ref_b, at):
        part = value.astype(bf16)
        ref_a[at] = part
        ref_b[at] = (value - part.astype(f32)).astype(bf16)

    for g in groups:
        def opaque(at):
            shade = op_live[:, at[1]] * jnp.exp(expo[at])
            alpha[at] = shade
            split_to(jnp.log(1.0 - shade), keep_a, keep_b, at)

        blocks(g, opaque)

    def total_of(ref_a, ref_b, cols):
        total = dot(ref_a[:, cols], ones) + dot(ref_b[:, cols], ones)
        return jnp.concatenate([total, total], axis=1)

    carried = None
    for g in groups:
        cols = slice(GROUP * g, GROUP * (g + 1))
        inside = dot(keep_a[:, cols], earlier) + dot(keep_b[:, cols], earlier)
        before[:, cols] = inside if carried is None else inside + carried
        if g + 1 < len(groups):
            total = total_of(keep_a, keep_b, cols)
            carried = total if carried is None else carried + total

    for g in groups:
        def weigh(at):
            weight = alpha[at] * jnp.exp(before[at])
            split_to(weight, weight_a, weight_b, at)
            weighted = gain[at] * weight
            wgain[at] = weighted
            split_to(weighted, keep_a, keep_b, at)

        blocks(g, weigh)

    carried = None
    for g in reversed(groups):
        cols = slice(GROUP * g, GROUP * (g + 1))
        inside = dot(keep_a[:, cols], later) + dot(keep_b[:, cols], later)
        behind[:, cols] = inside if carried is None else inside + carried
        if g:
            total = total_of(keep_a, keep_b, cols)
            carried = total if carried is None else carried + total

    for g in groups:
        def drop(at):
            shade = alpha[at]
            split_to(wgain[at] - behind[at] * (shade / (1.0 - shade)), drop_a, drop_b, at)

        blocks(g, drop)

    tint = dot(cot_rows, weight_a[...]) + dot(cot_rows, weight_b[...])
    tint = tint[0:8] + tint[8:16]
    moment = dot(basis_rows, drop_a[...]) + dot(basis_rows, drop_b[...])
    m_xx, m_yy, m_xy = moment[0:1], moment[1:2], moment[2:3]
    m_x, m_y, m_one = moment[3:4], moment[4:5], moment[5:6]
    m_du = m_x - off_x * m_one
    m_dv = m_y - off_y * m_one
    slot_grad = stack_rows(
        [
            con_a * m_du + con_b * m_dv,
            con_c * m_dv + con_b * m_du,
            -0.5 * (m_xx - off_x * (m_x + m_du)),
            -(m_xy - off_x * m_y - off_y * m_du),
            -0.5 * (m_yy - off_y * (m_y + m_dv)),
            m_one,
        ],
        8,
    )
    slot_grad = jnp.concatenate([slot_grad, tint], axis=0)

    spread = jnp.concatenate(
        [jnp.where(slot_part == s, slot_grad, 0.0) for s in range(8)], axis=0
    )
    sums = None
    for part in parts_of(spread, 3):
        term = dot(at_owner[...], part.astype(bf16), ((1,), (1,)))
        sums = term if sums is None else sums + term
    grad_out[:, 0, :] = sums
    exchange(grad_out, grad_in, sems[4], sems[5], lambda peer: peer)
    grad_in[me] = grad_out[me]
    wait_for(grad_in.at[pl.ds(0, N_TILE - 1)], sems[5])

    back = jnp.transpose(grad_in[:, 0, :])
    back = jnp.concatenate([back[16 * s : 16 * (s + 1)] for s in range(8)], axis=1)
    back = jnp.concatenate(parts_of(back, 3), axis=0).astype(bf16)
    back = dot(back, picked[...], ((1,), (1,)))
    back = back[0:16] + back[16:32] + back[32:48]
    cam_out[0:16] = back
    cam_out[16:24] = cam_rows

    for i in range(1, N_CAM):
        pltpu.make_async_remote_copy(
            cam_out, out_ref.at[cam], sems[6], sems[7],
            device_id=(me, lax.rem(cam + i, N_CAM)), device_id_type=MESH,
        ).start()
    out_ref[cam] = cam_out[...]
    wait_for(out_ref.at[pl.ds(0, N_CAM - 1)], sems[7])
    wait_for(out_ref.at[pl.ds(0, N_CAM - 1)], sems[6])
    for sem in (sems[0], sems[2], sems[4]):
        wait_for(row_in.at[pl.ds(0, N_TILE - 1)], sem)


def update_kernel(gauss_ref, one_ref, two_ref, back_ref, grad_ref, new_ref, first_ref, second_ref):
    rows = [gauss_ref[i : i + 1, :] for i in range(59)]
    cams = [back_ref[:, 16 + i, :] for i in range(5)]

    def values_of(wanted):
        full = [*wanted[:10], None, *wanted[10:]]
        return screen_of(full, cams[:3], cams[3], cams[4])

    wanted = [*rows[:10], *rows[11:]]
    _, pull = jax.vjp(values_of, wanted)
    order = [0, 1, 2, 3, 4, 8, 9, 10]
    (grads,) = pull([back_ref[:, i, :] for i in order])
    opacity = 1.0 / (1.0 + jnp.exp(-rows[10]))
    shade = jnp.sum(back_ref[:, 5, :], axis=0, keepdims=True) * (1.0 - opacity)
    for i, grad in enumerate([*grads[:10], shade, *grads[10:]]):
        grad_ref[i : i + 1, :] = grad
    grad = grad_ref[...]
    first = 0.9 * one_ref[...] + 0.1 * grad
    second = 0.999 * two_ref[...] + 0.001 * grad * grad
    first_ref[...] = first
    second_ref[...] = second
    new_ref[...] = gauss_ref[...] - 0.01 * first / (jnp.sqrt(second) + 1e-08)


def body(gaussians, moment_one, moment_two, cameras, requests, tile_lists, tile_lengths, cotangent):
    vmem = pl.BlockSpec(memory_space=pltpu.VMEM)
    message = (N_TILE, 1, 128)
    plane = (PIX, SLOTS)
    back = pl.pallas_call(
        splat_kernel,
        out_shape=jax.ShapeDtypeStruct((N_CAM, 24, OWN), f32),
        in_specs=[vmem] * 6,
        out_specs=vmem,
        scratch_shapes=[
            pltpu.VMEM((8, 1, 128), jnp.int32),
            pltpu.VMEM(message, jnp.int32),
            pltpu.VMEM(message, f32),
            pltpu.VMEM(message, f32),
            pltpu.VMEM(message, f32),
            pltpu.VMEM(message, f32),
            pltpu.VMEM((24, OWN), f32),
            pltpu.VMEM((OWN, SLOTS), bf16),
            pltpu.VMEM((N_TILE, SLOTS), bf16),
            pltpu.VMEM(plane, f32),
            pltpu.VMEM(plane, f32),
            pltpu.VMEM(plane, f32),
            pltpu.VMEM(plane, bf16),
            pltpu.VMEM(plane, bf16),
            pltpu.VMEM(plane, f32),
            pltpu.VMEM(plane, bf16),
            pltpu.VMEM(plane, bf16),
            pltpu.VMEM(plane, bf16),
            pltpu.VMEM(plane, bf16),
            pltpu.VMEM(plane, f32),
            pltpu.VMEM(plane, f32),
            pltpu.VMEM((128, 128), jnp.int32),
        ]
        + [pltpu.SemaphoreType.DMA] * 8,
        compiler_params=pltpu.CompilerParams(
            collective_id=0, has_side_effects=True, vmem_limit_bytes=40 * 1024 * 1024
        ),
        name="splat",
    )(gaussians, cameras, requests, tile_lists, tile_lengths, cotangent)
    leaf = jax.ShapeDtypeStruct(gaussians.shape, f32)
    return pl.pallas_call(
        update_kernel,
        out_shape=(leaf, leaf, leaf, leaf),
        in_specs=[vmem] * 4,
        out_specs=(vmem, vmem, vmem, vmem),
        compiler_params=pltpu.CompilerParams(vmem_limit_bytes=32 * 1024 * 1024),
        name="update",
    )(gaussians, moment_one, moment_two, back)


def solution(mesh):
    return jax.shard_map(
        body,
        mesh=mesh,
        in_specs=(
            P(None, "tile"),
            P(None, "tile"),
            P(None, "tile"),
            P("cam", None),
            P("cam", "tile"),
            P("cam", "tile", None),
            P("cam", "tile"),
            P("cam", "tile", None, None),
        ),
        out_specs=(P(None, "tile"), P(None, "tile"), P(None, "tile"), P(None, "tile")),
        check_vma=False,
    )
```

profile of v0, /device:TPU:1, one launch (start us, length us, event | category | flops | bytes accessed | tf_op | source)
XLA Modules:
  0.0 54.9 jit_solution(16530467893804061380)
XLA Ops:
  0.6 0.0 copy-start.4
  0.6 0.0 copy-start.3
  1.3 0.0 copy-start.5
  1.3 0.7 %copy.12.cot_ref = f32[1,1,3,256]{3,2,1,0:T(4,128)S(1)} copy(f32[1,1,3,256]{3,1,2,0:T(1,128)} %param.15) | data formatting | bytes 6144 | tf_op args[7]
  2.0 0.0 copy-done.4
  2.0 0.0 copy-done.3
  2.0 0.0 copy-done.5
  2.0 0.0 copy-start
  2.0 0.9 %copy-done = f32[59,512]{1,0:T(8,128)S(1)} copy-done((f32[59,512]{1,0:T(8,128)S(1)}, f32[59,512]{1,0:T(8,128)}, u32[]{:S(2)}) %copy-start) | copy-done | bytes 120856
  2.9 0.0 copy-start.1
  2.9 0.0 copy-start.2
  2.9 50.4 %splat.1.back_ref = f32[4,24,512]{2,1,0:T(8,128)S(1)} custom-call(f32[59,512]{1,0:T(8,128)S(1)} %copy-done, f32[1,4]{1,0:T(1,128)S(1)} %copy-done.5, s32[1,1024]{1,0:T(1,128)S(1)} %copy-done.3, s32[1,1,1024]{2,1,0:T(1,128)S(1)} %copy-done.4, s32[1,1]{1,0:T(1,128)S(6)} %copy.13.length_ref, f32[1,1,3,256]{3,2,1,0:T(4,128)S(1)} %copy.12.cot_ref), custom_call_target="tpu_custom_call" | custom-call | tf_op jit(solution)/shard_map/splat/pallas_call | solution.py:434
  53.4 0.0 copy-done.1
  53.4 0.0 copy-done.2
  53.4 1.5 %update.1 = (f32[59,512]{1,0:T(8,128)}, f32[59,512]{1,0:T(8,128)}, f32[59,512]{1,0:T(8,128)}, f32[59,512]{1,0:T(8,128)}) custom-call(f32[59,512]{1,0:T(8,128)S(1)} %copy-done, f32[59,512]{1,0:T(8,128)S(1)} %copy-done.1, f32[59,512]{1,0:T(8,128)S(1)} %copy-done.2, f32[4,24,512]{2,1,0:T(8,128)S(1)} %splat.1.back_ref), custom_call_target="tpu_custom_call" | custom-call | tf_op jit(solution)/shard_map/update/pallas_call | solution.py:470
Async XLA Ops:
  0.6 1.4 %copy-start.4 = (s32[1,1,1024]{2,1,0:T(1,128)S(1)}, s32[1,1,1024]{2,1,0:T(1,128)}, u32[]{:S(2)}) copy-start(s32[1,1,1024]{2,1,0:T(1,128)} %list_ref.1) | copy-start | bytes 12292
  0.6 1.4 %copy-start.3 = (s32[1,1024]{1,0:T(1,128)S(1)}, s32[1,1024]{1,0:T(1,128)}, u32[]{:S(2)}) copy-start(s32[1,1024]{1,0:T(1,128)} %req_ref.1) | copy-start | bytes 12292
  1.3 0.7 %copy-start.5 = (f32[1,4]{1,0:T(1,128)S(1)}, f32[1,4]{1,0:T(1,128)}, u32[]{:S(2)}) copy-start(f32[1,4]{1,0:T(1,128)} %camera_ref.1) | copy-start | bytes 52
  2.0 0.9 %copy-start = (f32[59,512]{1,0:T(8,128)S(1)}, f32[59,512]{1,0:T(8,128)}, u32[]{:S(2)}) copy-start(f32[59,512]{1,0:T(8,128)} %gauss_ref.3) | copy-start | bytes 362500
  2.9 50.4 %copy-start.1 = (f32[59,512]{1,0:T(8,128)S(1)}, f32[59,512]{1,0:T(8,128)}, u32[]{:S(2)}) copy-start(f32[59,512]{1,0:T(8,128)} %one_ref.1) | copy-start | bytes 362500
  2.9 50.5 %copy-start.2 = (f32[59,512]{1,0:T(8,128)S(1)}, f32[59,512]{1,0:T(8,128)}, u32[]{:S(2)}) copy-start(f32[59,512]{1,0:T(8,128)} %two_ref.1) | copy-start | bytes 362500
where the time goes:
time: 55.1 us; the launch traced here: 54.9 us
  Pallas kernels  52 us (94%)
  local copies, waits for them, and re-layouts  1.61 us (3%)
  between operations  1.36 us (2%)
    pallas_call x1, Pallas kernels, body(): pl.pallas_call(splat_kernel, out_shape=jax.ShapeDtypeStruct((N_CAM, 24, O...  50.4 us
    unnamed x13, local copies, waits for them, and re-layouts  1.61 us
    pallas_call x1, Pallas kernels, body(): pl.pallas_call(update_kernel, out_shape=(leaf, leaf, leaf, leaf), in_spec...  1.52 us

commit v1 on v0

--- a/solution.py
+++ b/solution.py
@@ -154,8 +154,9 @@
 
 
 def splat_kernel(
+    gauss_any, camera_any, req_any, list_any, length_any, cot_any,
+    out_ref,
     gauss_ref, camera_ref, req_ref, list_ref, length_ref, cot_ref,
-    out_ref,
     ask_out, ask_in, row_out, row_in, grad_out, grad_in, cam_out,
     picked, at_owner, expo, gain, alpha, keep_a, keep_b, before, weight_a, weight_b,
     drop_a, drop_b, behind, wgain, turned,
@@ -166,28 +167,48 @@
     high = me // 16
     low = lax.rem(me, 16)
 
+    def peers(action):
+        for step in (4, 3, 5, 2, 6, 1, 7, 0):
+            row = jnp.bitwise_and(high + step, 7)
+            for start, end in ((8, 16), (0, 8)) if step else ((8, 16), (1, 8)):
+
+                @pl.loop(start, end)
+                def _(i):
+                    action(row * 16 + jnp.bitwise_and(low + i, 15), row)
+
     barrier = pltpu.get_barrier_semaphore()
-
-    @pl.loop(1, N_TILE)
-    def _(i):
-        pl.semaphore_signal(
-            barrier, inc=1, device_id=(lax.rem(me + i, N_TILE), cam), device_id_type=MESH
+    peers(
+        lambda peer, row: pl.semaphore_signal(
+            barrier, inc=1, device_id=(peer, cam), device_id_type=MESH
         )
-
+    )
     for i in range(1, N_CAM):
         pl.semaphore_signal(
             barrier, inc=1, device_id=(me, lax.rem(cam + i, N_CAM)), device_id_type=MESH
         )
-
-    def exchange(src, dst, send_sem, recv_sem, source_of):
-        @pl.loop(1, N_TILE)
-        def _(i):
-            peer = lax.rem(me + i, N_TILE)
+    loads = [
+        pltpu.make_async_copy(src, dst, sem)
+        for src, dst, sem in zip(
+            (gauss_any, camera_any, req_any, list_any, length_any, cot_any),
+            (gauss_ref, camera_ref, req_ref, list_ref, length_ref, cot_ref),
+            sems[8:14],
+            strict=True,
+        )
+    ]
+    for load in loads:
+        load.start()
+
+    def exchange(src, dst, send_sem, recv_sem, by_row=False):
+        def send(peer, row):
             pltpu.make_async_remote_copy(
-                src.at[source_of(peer)], dst.at[me], send_sem, recv_sem,
+                src.at[row if by_row else peer], dst.at[me], send_sem, recv_sem,
                 device_id=(peer, cam), device_id_type=MESH,
             ).start()
 
+        peers(send)
+
+    for load in loads:
+        load.wait()
     for z in range(8):
         ask_out[z] = req_ref[:, 128 * z : 128 * (z + 1)]
     camera = camera_ref[...]
@@ -209,10 +230,10 @@
     )
 
     pl.semaphore_wait(barrier, N_TILE - 1 + N_CAM - 1)
-    exchange(ask_out, ask_in, sems[0], sems[1], lambda peer: peer // 16)
+    exchange(ask_out, ask_in, sems[0], sems[1], by_row=True)
     ask_in[me] = ask_out[high]
 
-    list_row = list_ref[0]
+    list_row = list_ref[...]
     slot_owner = lax.shift_right_logical(list_row, 3)
     slot_part = jnp.bitwise_and(list_row, 7)
     at_owner[...] = jnp.where(
@@ -227,7 +248,7 @@
     basis = stack_rows(
         [loc_x * loc_x, loc_y * loc_y, loc_x * loc_y, loc_x, loc_y, jnp.ones_like(loc_x)], 8
     )
-    cot = jnp.concatenate([cot_ref[0, 0], jnp.zeros((5, PIX), f32)], axis=0)
+    cot = stack_rows([cot_ref[0], cot_ref[1], cot_ref[2]], 8)
     cot_h, cot_m, cot_l = parts_of(cot, 3)
     wide = jnp.concatenate(
         [basis, basis, basis, cot_h, cot_h, cot_h, cot_m, cot_m, cot_l, jnp.zeros((56, PIX), f32)],
@@ -258,7 +279,7 @@
     found = found[0:16] + found[16:32] + found[32:48]
     found = jnp.concatenate([found[:, 128 * s : 128 * (s + 1)] for s in range(8)], axis=0)
     row_out[:, 0, :] = jnp.transpose(found)
-    exchange(row_out, row_in, sems[2], sems[3], lambda peer: peer)
+    exchange(row_out, row_in, sems[2], sems[3])
     row_in[me] = row_out[me]
     wait_for(row_in.at[pl.ds(0, N_TILE - 1)], sems[3])
 
@@ -375,19 +396,19 @@
         [jnp.where(slot_part == s, slot_grad, 0.0) for s in range(8)], axis=0
     )
     sums = None
-    for part in parts_of(spread, 3):
+    for part in parts_of(spread, 2):
         term = dot(at_owner[...], part.astype(bf16), ((1,), (1,)))
         sums = term if sums is None else sums + term
     grad_out[:, 0, :] = sums
-    exchange(grad_out, grad_in, sems[4], sems[5], lambda peer: peer)
+    exchange(grad_out, grad_in, sems[4], sems[5])
     grad_in[me] = grad_out[me]
     wait_for(grad_in.at[pl.ds(0, N_TILE - 1)], sems[5])
 
     back = jnp.transpose(grad_in[:, 0, :])
     back = jnp.concatenate([back[16 * s : 16 * (s + 1)] for s in range(8)], axis=1)
-    back = jnp.concatenate(parts_of(back, 3), axis=0).astype(bf16)
+    back = jnp.concatenate(parts_of(back, 2), axis=0).astype(bf16)
     back = dot(back, picked[...], ((1,), (1,)))
-    back = back[0:16] + back[16:32] + back[32:48]
+    back = back[0:16] + back[16:32]
     cam_out[0:16] = back
     cam_out[16:24] = cam_rows
 
@@ -403,7 +424,11 @@
         wait_for(row_in.at[pl.ds(0, N_TILE - 1)], sem)
 
 
-def update_kernel(gauss_ref, one_ref, two_ref, back_ref, grad_ref, new_ref, first_ref, second_ref):
+def update_kernel(
+    gauss_ref, one_ref, two_any, back_ref, grad_ref, new_ref, first_ref, second_ref, two_ref, sem
+):
+    load = pltpu.make_async_copy(two_any, two_ref, sem)
+    load.start()
     rows = [gauss_ref[i : i + 1, :] for i in range(59)]
     cams = [back_ref[:, 16 + i, :] for i in range(5)]
 
@@ -419,6 +444,7 @@
     shade = jnp.sum(back_ref[:, 5, :], axis=0, keepdims=True) * (1.0 - opacity)
     for i, grad in enumerate([*grads[:10], shade, *grads[10:]]):
         grad_ref[i : i + 1, :] = grad
+    load.wait()
     grad = grad_ref[...]
     first = 0.9 * one_ref[...] + 0.1 * grad
     second = 0.999 * two_ref[...] + 0.001 * grad * grad
@@ -427,16 +453,26 @@
     new_ref[...] = gauss_ref[...] - 0.01 * first / (jnp.sqrt(second) + 1e-08)
 
 
+def pin(value):
+    return pltpu.with_memory_space_constraint(value, pltpu.HBM)
+
+
 def body(gaussians, moment_one, moment_two, cameras, requests, tile_lists, tile_lengths, cotangent):
     vmem = pl.BlockSpec(memory_space=pltpu.VMEM)
     message = (N_TILE, 1, 128)
     plane = (PIX, SLOTS)
     back = pl.pallas_call(
         splat_kernel,
-        out_shape=jax.ShapeDtypeStruct((N_CAM, 24, OWN), f32),
-        in_specs=[vmem] * 6,
+        out_shape=pltpu.VMEM((N_CAM, 24, OWN), f32),
+        in_specs=[pl.BlockSpec(memory_space=pltpu.HBM)] * 6,
         out_specs=vmem,
         scratch_shapes=[
+            pltpu.VMEM(gaussians.shape, f32),
+            pltpu.VMEM((1, 4), f32),
+            pltpu.VMEM((1, SLOTS), jnp.int32),
+            pltpu.VMEM((1, SLOTS), jnp.int32),
+            pltpu.VMEM((1, 1), jnp.int32),
+            pltpu.VMEM((3, 1, PIX), f32),
             pltpu.VMEM((8, 1, 128), jnp.int32),
             pltpu.VMEM(message, jnp.int32),
             pltpu.VMEM(message, f32),
@@ -460,21 +496,25 @@
             pltpu.VMEM(plane, f32),
             pltpu.VMEM((128, 128), jnp.int32),
         ]
-        + [pltpu.SemaphoreType.DMA] * 8,
+        + [pltpu.SemaphoreType.DMA] * 14,
         compiler_params=pltpu.CompilerParams(
             collective_id=0, has_side_effects=True, vmem_limit_bytes=40 * 1024 * 1024
         ),
         name="splat",
-    )(gaussians, cameras, requests, tile_lists, tile_lengths, cotangent)
+    )(
+        pin(gaussians), pin(cameras), pin(requests), pin(tile_lists.reshape(1, SLOTS)),
+        tile_lengths, pin(cotangent.reshape(3, 1, PIX)),
+    )
     leaf = jax.ShapeDtypeStruct(gaussians.shape, f32)
     return pl.pallas_call(
         update_kernel,
         out_shape=(leaf, leaf, leaf, leaf),
-        in_specs=[vmem] * 4,
+        in_specs=[vmem, vmem, pl.BlockSpec(memory_space=pltpu.HBM), vmem],
         out_specs=(vmem, vmem, vmem, vmem),
+        scratch_shapes=[pltpu.VMEM(gaussians.shape, f32), pltpu.SemaphoreType.DMA],
         compiler_params=pltpu.CompilerParams(vmem_limit_bytes=32 * 1024 * 1024),
         name="update",
-    )(gaussians, moment_one, moment_two, back)
+    )(gaussians, moment_one, pin(moment_two), back)
 
 
 def solution(mesh):

time: 55.1 us -> 50.4 us (0.915)
  Pallas kernels: 52 us -> 48.9 us
  local copies, waits for them, and re-layouts: 1.61 us -> 0.01 us
    pallas_call x1, Pallas kernels: 50.4 us -> 47.1 us  [body(): pl.pallas_call(splat_kernel, out_shape=pltpu.VMEM((N_CAM, 24, OWN), f32),...]
    unnamed x13 -> x4, local copies, waits for them, and re-layouts: 1.61 us -> 0.01 us
where the time goes in v1:
time: 50.4 us; the launch traced here: 50.2 us
  Pallas kernels  48.9 us (97%)
  between operations  1.32 us (3%)
    pallas_call x1, Pallas kernels, body(): pl.pallas_call(splat_kernel, out_shape=pltpu.VMEM((N_CAM, 24, OWN), f32),...  47.1 us
    pallas_call x1, Pallas kernels, body(): pl.pallas_call(update_kernel, out_shape=(leaf, leaf, leaf, leaf), in_spec...  1.73 us

profile of v1, /device:TPU:1, one launch (start us, length us, event | category | flops | bytes accessed | tf_op | source)
XLA Modules:
  0.0 50.2 jit_solution(4641229560560448117)
XLA Ops:
  1.3 0.0 copy-start
  1.3 0.0 copy-start.1
  1.3 47.1 %splat.1.back_ref = f32[4,24,512]{2,1,0:T(8,128)S(1)} custom-call(f32[59,512]{1,0:T(8,128)} %gauss_ref.1, f32[1,4]{1,0:T(1,128)} %camera_any.1, s32[1,1024]{1,0:T(1,128)} %req_any.1, s32[1,1024]{1,0:T(1,128)} %bitcast.2, s32[1,1]{1,0:T(1,128)S(6)} %copy.12.length_any, f32[3,1,256]{2,1,0:T(1,128)} %bitcast.3), custom_call_target="tpu_custom_call" | custom-call | tf_op jit(solution)/shard_map/splat/pallas_call | solution.py:464
  48.4 0.0 copy-done
  48.5 0.0 copy-done.1
  48.5 1.7 %update.1 = (f32[59,512]{1,0:T(8,128)}, f32[59,512]{1,0:T(8,128)}, f32[59,512]{1,0:T(8,128)}, f32[59,512]{1,0:T(8,128)}) custom-call(f32[59,512]{1,0:T(8,128)S(1)} %copy-done, f32[59,512]{1,0:T(8,128)S(1)} %copy-done.1, f32[59,512]{1,0:T(8,128)} %two_any.1, f32[4,24,512]{2,1,0:T(8,128)S(1)} %splat.1.back_ref), custom_call_target="tpu_custom_call" | custom-call | tf_op jit(solution)/shard_map/update/pallas_call | solution.py:509
Async XLA Ops:
  1.3 47.2 %copy-start = (f32[59,512]{1,0:T(8,128)S(1)}, f32[59,512]{1,0:T(8,128)}, u32[]{:S(2)}) copy-start(f32[59,512]{1,0:T(8,128)} %gauss_ref.1) | copy-start | bytes 362500
  1.3 47.2 %copy-start.1 = (f32[59,512]{1,0:T(8,128)S(1)}, f32[59,512]{1,0:T(8,128)}, u32[]{:S(2)}) copy-start(f32[59,512]{1,0:T(8,128)} %one_ref.1) | copy-start | bytes 362500

commit v2 on v1

--- a/solution.py
+++ b/solution.py
@@ -14,7 +14,6 @@
 SLOTS = 1024
 PIX = 256
 GROUP = 256
-SHIFT = 32
 
 focal_length = 350.0
 dilation = 0.3
@@ -159,7 +158,7 @@
     gauss_ref, camera_ref, req_ref, list_ref, length_ref, cot_ref,
     ask_out, ask_in, row_out, row_in, grad_out, grad_in, cam_out,
     picked, at_owner, expo, gain, alpha, keep_a, keep_b, before, weight_a, weight_b,
-    drop_a, drop_b, behind, wgain, turned,
+    drop_a, drop_b, behind, wgain, turned, at_owner_t, picked_t,
     *sems,
 ):
     me = lax.axis_index("tile")
@@ -222,12 +221,17 @@
     opacity = 1.0 / (1.0 + jnp.exp(-rows[10]))
     zero = jnp.zeros_like(opacity)
     table = stack_rows([*values[:5], opacity, zero, zero, *values[5:]], 16)
-    table = jnp.concatenate(parts_of(table, 3), axis=0).astype(bf16)
-    cam_rows = stack_rows(
-        [jnp.broadcast_to(v, (1, OWN)) for v in
-         (camera[:, 0:1], camera[:, 1:2], camera[:, 2:3], cos_yaw, sin_yaw)],
-        8,
-    )
+    table = jnp.concatenate(
+        [part[:, 128 * c : 128 * (c + 1)] for part in parts_of(table, 3) for c in range(OWN // 128)],
+        axis=0,
+    ).astype(bf16)
+    lane = lax.broadcasted_iota(jnp.int32, (1, OWN), 1)
+    cam_row = jnp.zeros((1, OWN), f32)
+    for i, value in enumerate(
+        (camera[:, 0:1], camera[:, 1:2], camera[:, 2:3], cos_yaw, sin_yaw)
+    ):
+        cam_row = jnp.where(lane == i, value, cam_row)
+    cam_out[9] = cam_row
 
     pl.semaphore_wait(barrier, N_TILE - 1 + N_CAM - 1)
     exchange(ask_out, ask_in, sems[0], sems[1], by_row=True)
@@ -236,12 +240,15 @@
     list_row = list_ref[...]
     slot_owner = lax.shift_right_logical(list_row, 3)
     slot_part = jnp.bitwise_and(list_row, 7)
-    at_owner[...] = jnp.where(
+    of_owner = jnp.where(
         lax.broadcasted_iota(jnp.int32, (N_TILE, SLOTS), 0) == slot_owner, 1.0, 0.0
-    ).astype(bf16)
+    )
+    for i in range(3):
+        at_owner[N_TILE * i : N_TILE * (i + 1), :] = of_owner.astype(bf16)
     live = (
         lax.broadcasted_iota(jnp.int32, (1, SLOTS), 1) < jnp.broadcast_to(length_ref[...], (1, SLOTS))
     )
+    at_owner_t[...] = jnp.transpose(of_owner).astype(bf16)
     pixel = lax.broadcasted_iota(jnp.int32, (1, PIX), 1)
     loc_x = jnp.bitwise_and(pixel, 15).astype(f32) - 7.5
     loc_y = lax.shift_right_logical(pixel, 4).astype(f32) - 7.5
@@ -270,23 +277,29 @@
     asked = jnp.transpose(ask_in[:, 0, :])
     turned[...] = asked
     asked = turned[pl.ds(pl.multiple_of(low * 8, 8), 8), :]
-    own_at = lax.broadcasted_iota(jnp.int32, (OWN, 128), 0)
+    fine_at = lax.broadcasted_iota(jnp.int32, (128, 128), 0)
+    coarse = lax.shift_right_logical(asked, 7)
+    coarse = jnp.concatenate([coarse[s : s + 1] for s in range(8)], axis=1)
+    asked = jnp.bitwise_and(asked, 127)
     for s in range(8):
         picked[:, 128 * s : 128 * (s + 1)] = jnp.where(
-            own_at == asked[s : s + 1, :], 1.0, 0.0
+            fine_at == asked[s : s + 1, :], 1.0, 0.0
         ).astype(bf16)
     found = dot(table, picked[...])
-    found = found[0:16] + found[16:32] + found[32:48]
+    found = found[0:64] + found[64:128] + found[128:192]
+    found = sum(
+        jnp.where(coarse == c, found[16 * c : 16 * (c + 1)], 0.0) for c in range(OWN // 128)
+    )
     found = jnp.concatenate([found[:, 128 * s : 128 * (s + 1)] for s in range(8)], axis=0)
     row_out[:, 0, :] = jnp.transpose(found)
     exchange(row_out, row_in, sems[2], sems[3])
     row_in[me] = row_out[me]
+    picked_t[...] = jnp.transpose(picked[...].astype(f32)).astype(bf16)
     wait_for(row_in.at[pl.ds(0, N_TILE - 1)], sems[3])
 
     got = jnp.transpose(row_in[:, 0, :])
-    got = jnp.concatenate(parts_of(got, 3), axis=0).astype(bf16)
+    got = jnp.concatenate(parts_of(got, 3), axis=1).astype(bf16)
     listed = dot(got, at_owner[...])
-    listed = listed[0:128] + listed[128:256] + listed[256:384]
     slot = jnp.zeros((16, SLOTS), f32)
     for s in range(8):
         slot = slot + jnp.where(slot_part == s, listed[16 * s : 16 * (s + 1)], 0.0)
@@ -314,11 +327,7 @@
     groups = range(SLOTS // GROUP)
 
     def blocks(group, step):
-        cols = slice(GROUP * group, GROUP * (group + 1))
-
-        @pl.loop(0, PIX // SHIFT)
-        def _(i):
-            step((pl.ds(pl.multiple_of(i * SHIFT, SHIFT), SHIFT), cols))
+        step((slice(None), slice(GROUP * group, GROUP * (group + 1))))
 
     def split_to(value, ref_a, ref_b, at):
         part = value.astype(bf16)
@@ -395,10 +404,9 @@
     spread = jnp.concatenate(
         [jnp.where(slot_part == s, slot_grad, 0.0) for s in range(8)], axis=0
     )
-    sums = None
-    for part in parts_of(spread, 2):
-        term = dot(at_owner[...], part.astype(bf16), ((1,), (1,)))
-        sums = term if sums is None else sums + term
+    spread = jnp.concatenate(parts_of(spread, 2), axis=0).astype(bf16)
+    sums = dot(spread, at_owner_t[...])
+    sums = jnp.transpose(sums[0:128] + sums[128:256])
     grad_out[:, 0, :] = sums
     exchange(grad_out, grad_in, sems[4], sems[5])
     grad_in[me] = grad_out[me]
@@ -406,11 +414,17 @@
 
     back = jnp.transpose(grad_in[:, 0, :])
     back = jnp.concatenate([back[16 * s : 16 * (s + 1)] for s in range(8)], axis=1)
-    back = jnp.concatenate(parts_of(back, 2), axis=0).astype(bf16)
-    back = dot(back, picked[...], ((1,), (1,)))
-    back = back[0:16] + back[16:32]
-    cam_out[0:16] = back
-    cam_out[16:24] = cam_rows
+    back = jnp.concatenate(parts_of(back, 2), axis=0)
+    back = jnp.concatenate(
+        [jnp.where(coarse == c, back, 0.0) for c in range(OWN // 128)], axis=0
+    ).astype(bf16)
+    back = dot(back, picked_t[...])
+    back = jnp.concatenate(
+        [back[32 * c : 32 * c + 16] + back[32 * c + 16 : 32 * (c + 1)] for c in range(OWN // 128)],
+        axis=1,
+    )
+    for i, at in enumerate((0, 1, 2, 3, 4, 5, 8, 9, 10)):
+        cam_out[i] = back[at : at + 1]
 
     for i in range(1, N_CAM):
         pltpu.make_async_remote_copy(
@@ -425,26 +439,46 @@
 
 
 def update_kernel(
-    gauss_ref, one_ref, two_any, back_ref, grad_ref, new_ref, first_ref, second_ref, two_ref, sem
+    gauss_ref, one_any, two_any, back_ref, grad_ref, new_ref, first_ref, second_ref,
+    one_ref, two_ref, *sems,
 ):
-    load = pltpu.make_async_copy(two_any, two_ref, sem)
-    load.start()
-    rows = [gauss_ref[i : i + 1, :] for i in range(59)]
-    cams = [back_ref[:, 16 + i, :] for i in range(5)]
+    loads = [
+        pltpu.make_async_copy(one_any, one_ref, sems[0]),
+        pltpu.make_async_copy(two_any, two_ref, sems[1]),
+    ]
+    for load in loads:
+        load.start()
+    half = OWN // 2
+    first_half = lax.broadcasted_iota(jnp.int32, (8, half), 0) < N_CAM
+
+    def spread(row):
+        return jnp.where(first_half, row[:, :half], row[:, half:])
+
+    def gathered(i):
+        values = back_ref[:, i, 0, :]
+        return jnp.concatenate([values[:, :half], values[:, half:]], axis=0)
+
+    def over_cams(grad):
+        return [jnp.sum(grad[at : at + N_CAM], axis=0, keepdims=True) for at in (0, N_CAM)]
+
+    rows = [spread(gauss_ref[i : i + 1, :]) for i in range(59)]
+    cam_rows = back_ref[:, 9, 0, 0:128]
+    cam_rows = jnp.concatenate([cam_rows, cam_rows], axis=0)
+    cams = [cam_rows[:, i : i + 1] for i in range(5)]
 
     def values_of(wanted):
         full = [*wanted[:10], None, *wanted[10:]]
         return screen_of(full, cams[:3], cams[3], cams[4])
 
-    wanted = [*rows[:10], *rows[11:]]
-    _, pull = jax.vjp(values_of, wanted)
-    order = [0, 1, 2, 3, 4, 8, 9, 10]
-    (grads,) = pull([back_ref[:, i, :] for i in order])
-    opacity = 1.0 / (1.0 + jnp.exp(-rows[10]))
-    shade = jnp.sum(back_ref[:, 5, :], axis=0, keepdims=True) * (1.0 - opacity)
+    _, pull = jax.vjp(values_of, [*rows[:10], *rows[11:]])
+    (grads,) = pull([gathered(i) for i in (0, 1, 2, 3, 4, 6, 7, 8)])
+    shade = gathered(5) * (1.0 - 1.0 / (1.0 + jnp.exp(-rows[10])))
     for i, grad in enumerate([*grads[:10], shade, *grads[10:]]):
-        grad_ref[i : i + 1, :] = grad
-    load.wait()
+        low, high = over_cams(grad)
+        grad_ref[i : i + 1, :half] = low
+        grad_ref[i : i + 1, half:] = high
+    for load in loads:
+        load.wait()
     grad = grad_ref[...]
     first = 0.9 * one_ref[...] + 0.1 * grad
     second = 0.999 * two_ref[...] + 0.001 * grad * grad
@@ -459,12 +493,13 @@
 
 def body(gaussians, moment_one, moment_two, cameras, requests, tile_lists, tile_lengths, cotangent):
     vmem = pl.BlockSpec(memory_space=pltpu.VMEM)
+    hbm = pl.BlockSpec(memory_space=pltpu.HBM)
     message = (N_TILE, 1, 128)
     plane = (PIX, SLOTS)
     back = pl.pallas_call(
         splat_kernel,
-        out_shape=pltpu.VMEM((N_CAM, 24, OWN), f32),
-        in_specs=[pl.BlockSpec(memory_space=pltpu.HBM)] * 6,
+        out_shape=pltpu.VMEM((N_CAM, 10, 1, OWN), f32),
+        in_specs=[hbm] * 6,
         out_specs=vmem,
         scratch_shapes=[
             pltpu.VMEM(gaussians.shape, f32),
@@ -479,9 +514,9 @@
             pltpu.VMEM(message, f32),
             pltpu.VMEM(message, f32),
             pltpu.VMEM(message, f32),
-            pltpu.VMEM((24, OWN), f32),
-            pltpu.VMEM((OWN, SLOTS), bf16),
-            pltpu.VMEM((N_TILE, SLOTS), bf16),
+            pltpu.VMEM((10, 1, OWN), f32),
+            pltpu.VMEM((128, SLOTS), bf16),
+            pltpu.VMEM((3 * N_TILE, SLOTS), bf16),
             pltpu.VMEM(plane, f32),
             pltpu.VMEM(plane, f32),
             pltpu.VMEM(plane, f32),
@@ -495,6 +530,8 @@
             pltpu.VMEM(plane, f32),
             pltpu.VMEM(plane, f32),
             pltpu.VMEM((128, 128), jnp.int32),
+            pltpu.VMEM((SLOTS, N_TILE), bf16),
+            pltpu.VMEM((SLOTS, 128), bf16),
         ]
         + [pltpu.SemaphoreType.DMA] * 14,
         compiler_params=pltpu.CompilerParams(
@@ -509,12 +546,12 @@
     return pl.pallas_call(
         update_kernel,
         out_shape=(leaf, leaf, leaf, leaf),
-        in_specs=[vmem, vmem, pl.BlockSpec(memory_space=pltpu.HBM), vmem],
+        in_specs=[vmem, hbm, hbm, vmem],
         out_specs=(vmem, vmem, vmem, vmem),
-        scratch_shapes=[pltpu.VMEM(gaussians.shape, f32), pltpu.SemaphoreType.DMA],
+        scratch_shapes=[pltpu.VMEM(gaussians.shape, f32)] * 2 + [pltpu.SemaphoreType.DMA] * 2,
         compiler_params=pltpu.CompilerParams(vmem_limit_bytes=32 * 1024 * 1024),
         name="update",
-    )(gaussians, moment_one, pin(moment_two), back)
+    )(gaussians, pin(moment_one), pin(moment_two), back)
 
 
 def solution(mesh):

time: 50.4 us -> 46.8 us (0.929)
  Pallas kernels: 48.9 us -> 45.3 us
    pallas_call x1, Pallas kernels: 47.1 us -> 43.5 us  [body(): pl.pallas_call(splat_kernel, out_shape=pltpu.VMEM((N_CAM, 10, 1, OWN), f3...]
where the time goes in v2:
time: 46.8 us; the launch traced here: 46.7 us
  Pallas kernels  45.3 us (97%)
  between operations  1.34 us (3%)
    pallas_call x1, Pallas kernels, body(): pl.pallas_call(splat_kernel, out_shape=pltpu.VMEM((N_CAM, 10, 1, OWN), f3...  43.5 us
    pallas_call x1, Pallas kernels, body(): pl.pallas_call(update_kernel, out_shape=(leaf, leaf, leaf, leaf), in_spec...  1.81 us

profile of v2, /device:TPU:1, one launch (start us, length us, event | category | flops | bytes accessed | tf_op | source)
XLA Modules:
  0.0 46.7 jit_solution(6147356350337747050)
XLA Ops:
  0.6 0.0 copy-start
  1.3 43.5 %splat.1.back_ref = f32[4,10,1,512]{3,2,1,0:T(1,128)S(1)} custom-call(f32[59,512]{1,0:T(8,128)} %gauss_ref.1, f32[1,4]{1,0:T(1,128)} %camera_any.1, s32[1,1024]{1,0:T(1,128)} %req_any.1, s32[1,1024]{1,0:T(1,128)} %bitcast.2, s32[1,1]{1,0:T(1,128)S(6)} %copy.12.length_any, f32[3,1,256]{2,1,0:T(1,128)} %bitcast.3), custom_call_target="tpu_custom_call" | custom-call | tf_op jit(solution)/shard_map/splat/pallas_call | solution.py:499
  44.8 0.0 copy-done
  44.9 1.8 %update.1 = (f32[59,512]{1,0:T(8,128)}, f32[59,512]{1,0:T(8,128)}, f32[59,512]{1,0:T(8,128)}, f32[59,512]{1,0:T(8,128)}) custom-call(f32[59,512]{1,0:T(8,128)S(1)} %copy-done, f32[59,512]{1,0:T(8,128)} %one_any.1, f32[59,512]{1,0:T(8,128)} %two_any.1, f32[4,10,1,512]{3,2,1,0:T(1,128)S(1)} %splat.1.back_ref), custom_call_target="tpu_custom_call" | custom-call | tf_op jit(solution)/shard_map/update/pallas_call | solution.py:546
Async XLA Ops:
  0.6 44.2 %copy-start = (f32[59,512]{1,0:T(8,128)S(1)}, f32[59,512]{1,0:T(8,128)}, u32[]{:S(2)}) copy-start(f32[59,512]{1,0:T(8,128)} %gauss_ref.1) | copy-start | bytes 362500

commit v3 on v2

--- a/solution.py
+++ b/solution.py
@@ -153,9 +153,9 @@
 
 
 def splat_kernel(
-    gauss_any, camera_any, req_any, list_any, length_any, cot_any,
-    out_ref,
-    gauss_ref, camera_ref, req_ref, list_ref, length_ref, cot_ref,
+    gauss_any, camera_any, req_any, list_any, length_any, cot_any, one_any, two_any,
+    out_ref, gauss_ref, one_ref, two_ref,
+    camera_ref, req_ref, list_ref, cot_ref,
     ask_out, ask_in, row_out, row_in, grad_out, grad_in, cam_out,
     picked, at_owner, expo, gain, alpha, keep_a, keep_b, before, weight_a, weight_b,
     drop_a, drop_b, behind, wgain, turned, at_owner_t, picked_t,
@@ -188,9 +188,9 @@
     loads = [
         pltpu.make_async_copy(src, dst, sem)
         for src, dst, sem in zip(
-            (gauss_any, camera_any, req_any, list_any, length_any, cot_any),
-            (gauss_ref, camera_ref, req_ref, list_ref, length_ref, cot_ref),
-            sems[8:14],
+            (gauss_any, camera_any, req_any, list_any, cot_any, one_any, two_any),
+            (gauss_ref, camera_ref, req_ref, list_ref, cot_ref, one_ref, two_ref),
+            sems[8:15],
             strict=True,
         )
     ]
@@ -206,7 +206,7 @@
 
         peers(send)
 
-    for load in loads:
+    for load in loads[:5]:
         load.wait()
     for z in range(8):
         ask_out[z] = req_ref[:, 128 * z : 128 * (z + 1)]
@@ -246,7 +246,7 @@
     for i in range(3):
         at_owner[N_TILE * i : N_TILE * (i + 1), :] = of_owner.astype(bf16)
     live = (
-        lax.broadcasted_iota(jnp.int32, (1, SLOTS), 1) < jnp.broadcast_to(length_ref[...], (1, SLOTS))
+        lax.broadcasted_iota(jnp.int32, (1, SLOTS), 1) < length_any[0, 0]
     )
     at_owner_t[...] = jnp.transpose(of_owner).astype(bf16)
     pixel = lax.broadcasted_iota(jnp.int32, (1, PIX), 1)
@@ -270,7 +270,6 @@
     down = lax.broadcasted_iota(jnp.int32, (GROUP, GROUP), 1)
     earlier = jnp.where(up < down, 1.0, 0.0).astype(bf16)
     later = jnp.where(up > down, 1.0, 0.0).astype(bf16)
-    ones = jnp.ones((GROUP, 128), bf16)
 
     wait_for(ask_in.at[pl.ds(0, N_TILE - 1)], sems[1])
 
@@ -342,18 +341,20 @@
 
         blocks(g, opaque)
 
-    def total_of(ref_a, ref_b, cols):
-        total = dot(ref_a[:, cols], ones) + dot(ref_b[:, cols], ones)
-        return jnp.concatenate([total, total], axis=1)
+    def edge_of(inside, ref_a, ref_b, at):
+        own = ref_a[:, at : at + 1].astype(f32) + ref_b[:, at : at + 1].astype(f32)
+        edge = at % GROUP
+        return jnp.broadcast_to(inside[:, edge : edge + 1] + own, (PIX, GROUP))
 
     carried = None
     for g in groups:
         cols = slice(GROUP * g, GROUP * (g + 1))
         inside = dot(keep_a[:, cols], earlier) + dot(keep_b[:, cols], earlier)
-        before[:, cols] = inside if carried is None else inside + carried
+        if carried is not None:
+            inside = inside + carried
+        before[:, cols] = inside
         if g + 1 < len(groups):
-            total = total_of(keep_a, keep_b, cols)
-            carried = total if carried is None else carried + total
+            carried = edge_of(inside, keep_a, keep_b, GROUP * (g + 1) - 1)
 
     for g in groups:
         def weigh(at):
@@ -369,10 +370,11 @@
     for g in reversed(groups):
         cols = slice(GROUP * g, GROUP * (g + 1))
         inside = dot(keep_a[:, cols], later) + dot(keep_b[:, cols], later)
-        behind[:, cols] = inside if carried is None else inside + carried
+        if carried is not None:
+            inside = inside + carried
+        behind[:, cols] = inside
         if g:
-            total = total_of(keep_a, keep_b, cols)
-            carried = total if carried is None else carried + total
+            carried = edge_of(inside, keep_a, keep_b, GROUP * g)
 
     for g in groups:
         def drop(at):
@@ -434,20 +436,13 @@
     out_ref[cam] = cam_out[...]
     wait_for(out_ref.at[pl.ds(0, N_CAM - 1)], sems[7])
     wait_for(out_ref.at[pl.ds(0, N_CAM - 1)], sems[6])
+    for load in loads[5:]:
+        load.wait()
     for sem in (sems[0], sems[2], sems[4]):
         wait_for(row_in.at[pl.ds(0, N_TILE - 1)], sem)
 
 
-def update_kernel(
-    gauss_ref, one_any, two_any, back_ref, grad_ref, new_ref, first_ref, second_ref,
-    one_ref, two_ref, *sems,
-):
-    loads = [
-        pltpu.make_async_copy(one_any, one_ref, sems[0]),
-        pltpu.make_async_copy(two_any, two_ref, sems[1]),
-    ]
-    for load in loads:
-        load.start()
+def update_kernel(gauss_ref, one_ref, two_ref, back_ref, grad_ref, new_ref, first_ref, second_ref):
     half = OWN // 2
     first_half = lax.broadcasted_iota(jnp.int32, (8, half), 0) < N_CAM
 
@@ -477,8 +472,6 @@
         low, high = over_cams(grad)
         grad_ref[i : i + 1, :half] = low
         grad_ref[i : i + 1, half:] = high
-    for load in loads:
-        load.wait()
     grad = grad_ref[...]
     first = 0.9 * one_ref[...] + 0.1 * grad
     second = 0.999 * two_ref[...] + 0.001 * grad * grad
@@ -496,17 +489,15 @@
     hbm = pl.BlockSpec(memory_space=pltpu.HBM)
     message = (N_TILE, 1, 128)
     plane = (PIX, SLOTS)
-    back = pl.pallas_call(
+    back, own, one, two = pl.pallas_call(
         splat_kernel,
-        out_shape=pltpu.VMEM((N_CAM, 10, 1, OWN), f32),
-        in_specs=[hbm] * 6,
-        out_specs=vmem,
+        out_shape=[pltpu.VMEM((N_CAM, 10, 1, OWN), f32)] + [pltpu.VMEM(gaussians.shape, f32)] * 3,
+        in_specs=[hbm, hbm, hbm, hbm, pl.BlockSpec(memory_space=pltpu.SMEM), hbm, hbm, hbm],
+        out_specs=[vmem] * 4,
         scratch_shapes=[
-            pltpu.VMEM(gaussians.shape, f32),
             pltpu.VMEM((1, 4), f32),
             pltpu.VMEM((1, SLOTS), jnp.int32),
             pltpu.VMEM((1, SLOTS), jnp.int32),
-            pltpu.VMEM((1, 1), jnp.int32),
             pltpu.VMEM((3, 1, PIX), f32),
             pltpu.VMEM((8, 1, 128), jnp.int32),
             pltpu.VMEM(message, jnp.int32),
@@ -533,25 +524,24 @@
             pltpu.VMEM((SLOTS, N_TILE), bf16),
             pltpu.VMEM((SLOTS, 128), bf16),
         ]
-        + [pltpu.SemaphoreType.DMA] * 14,
+        + [pltpu.SemaphoreType.DMA] * 15,
         compiler_params=pltpu.CompilerParams(
             collective_id=0, has_side_effects=True, vmem_limit_bytes=40 * 1024 * 1024
         ),
         name="splat",
     )(
         pin(gaussians), pin(cameras), pin(requests), pin(tile_lists.reshape(1, SLOTS)),
-        tile_lengths, pin(cotangent.reshape(3, 1, PIX)),
+        tile_lengths, pin(cotangent.reshape(3, 1, PIX)), pin(moment_one), pin(moment_two),
     )
     leaf = jax.ShapeDtypeStruct(gaussians.shape, f32)
     return pl.pallas_call(
         update_kernel,
         out_shape=(leaf, leaf, leaf, leaf),
-        in_specs=[vmem, hbm, hbm, vmem],
+        in_specs=[vmem] * 4,
         out_specs=(vmem, vmem, vmem, vmem),
-        scratch_shapes=[pltpu.VMEM(gaussians.shape, f32)] * 2 + [pltpu.SemaphoreType.DMA] * 2,
         compiler_params=pltpu.CompilerParams(vmem_limit_bytes=32 * 1024 * 1024),
         name="update",
-    )(gaussians, pin(moment_one), pin(moment_two), back)
+    )(own, one, two, back)
 
 
 def solution(mesh):

time: 46.8 us -> 46.1 us (0.985)
  Pallas kernels: 45.3 us -> 44.7 us
where the time goes in v3:
time: 46.1 us; the launch traced here: 46 us
  Pallas kernels  44.7 us (97%)
  between operations  1.29 us (3%)
    pallas_call x1, Pallas kernels, body(): pl.pallas_call(splat_kernel, out_shape=[pltpu.VMEM((N_CAM, 10, 1, OWN), f...  43.3 us
    pallas_call x1, Pallas kernels, body(): pl.pallas_call(update_kernel, out_shape=(leaf, leaf, leaf, leaf), in_spec...  1.37 us

profile of v3, /device:TPU:1, one launch (start us, length us, event | category | flops | bytes accessed | tf_op | source)
XLA Modules:
  0.0 46.0 jit_solution(14423519345273946776)
XLA Ops:
  1.3 43.3 %splat.1 = (f32[4,10,1,512]{3,2,1,0:T(1,128)S(1)}, f32[59,512]{1,0:T(8,128)S(1)}, f32[59,512]{1,0:T(8,128)S(1)}, f32[59,512]{1,0:T(8,128)S(1)}) custom-call(f32[59,512]{1,0:T(8,128)} %gauss_any.1, f32[1,4]{1,0:T(1,128)} %camera_any.1, s32[1,1024]{1,0:T(1,128)} %req_any.1, s32[1,1024]{1,0:T(1,128)} %bitcast.2, s32[1,1]{1,0:T(1,128)S(6)} %copy.12.length_any, ...), custom_call_target="tpu_custom_call" | custom-call | tf_op jit(solution)/shard_map/splat/pallas_call | solution.py:492
  44.6 1.4 %update.1 = (f32[59,512]{1,0:T(8,128)}, f32[59,512]{1,0:T(8,128)}, f32[59,512]{1,0:T(8,128)}, f32[59,512]{1,0:T(8,128)}) custom-call(f32[59,512]{1,0:T(8,128)S(1)} %get-tuple-element.8.gauss_ref, f32[59,512]{1,0:T(8,128)S(1)} %get-tuple-element.9.one_ref, f32[59,512]{1,0:T(8,128)S(1)} %get-tuple-element.10.two_ref, ...), custom_call_target="tpu_custom_call" | custom-call | tf_op jit(solution)/shard_map/update/pallas_call | solution.py:537

commit v4 on v3

--- a/solution.py
+++ b/solution.py
@@ -157,8 +157,8 @@
     out_ref, gauss_ref, one_ref, two_ref,
     camera_ref, req_ref, list_ref, cot_ref,
     ask_out, ask_in, row_out, row_in, grad_out, grad_in, cam_out,
-    picked, at_owner, expo, gain, alpha, keep_a, keep_b, before, weight_a, weight_b,
-    drop_a, drop_b, behind, wgain, turned, at_owner_t, picked_t,
+    picked, at_owner, gain, alpha, keep_a, keep_b, before, cot_wide,
+    behind, wgain, turned, at_owner_t, picked_t,
     *sems,
 ):
     me = lax.axis_index("tile")
@@ -249,23 +249,17 @@
         lax.broadcasted_iota(jnp.int32, (1, SLOTS), 1) < length_any[0, 0]
     )
     at_owner_t[...] = jnp.transpose(of_owner).astype(bf16)
-    pixel = lax.broadcasted_iota(jnp.int32, (1, PIX), 1)
-    loc_x = jnp.bitwise_and(pixel, 15).astype(f32) - 7.5
-    loc_y = lax.shift_right_logical(pixel, 4).astype(f32) - 7.5
-    basis = stack_rows(
-        [loc_x * loc_x, loc_y * loc_y, loc_x * loc_y, loc_x, loc_y, jnp.ones_like(loc_x)], 8
-    )
     cot = stack_rows([cot_ref[0], cot_ref[1], cot_ref[2]], 8)
     cot_h, cot_m, cot_l = parts_of(cot, 3)
     wide = jnp.concatenate(
-        [basis, basis, basis, cot_h, cot_h, cot_h, cot_m, cot_m, cot_l, jnp.zeros((56, PIX), f32)],
+        [cot_h, cot_h, cot_h, cot_m, cot_m, cot_l, cot, jnp.zeros((72, PIX), f32)],
         axis=0,
     )
-    wide = jnp.transpose(wide).astype(bf16)
-    basis_cols = wide[:, 0:24]
-    cot_cols = wide[:, 24:72]
-    cot_rows = jnp.concatenate([cot_h, cot_m], axis=0).astype(bf16)
-    basis_rows = jnp.concatenate([basis, jnp.zeros_like(basis)], axis=0).astype(bf16)
+    wide = jnp.transpose(wide)
+    for channel in range(3):
+        cot_wide[channel] = jnp.broadcast_to(wide[:, 48 + channel : 49 + channel], (PIX, 128))
+    wide = wide.astype(bf16)
+    cot_cols = wide[:, 0:48]
     up = lax.broadcasted_iota(jnp.int32, (GROUP, GROUP), 0)
     down = lax.broadcasted_iota(jnp.int32, (GROUP, GROUP), 1)
     earlier = jnp.where(up < down, 1.0, 0.0).astype(bf16)
@@ -308,22 +302,14 @@
     off_y = slot[1:2] - tile_y
     con_a, con_b, con_c = slot[2:3], slot[3:4], slot[4:5]
     op_live = jnp.where(live, slot[5:6], 0.0)
-    push_x = con_a * off_x + con_b * off_y
-    push_y = con_c * off_y + con_b * off_x
-    coef = stack_rows(
-        [-0.5 * con_a, -0.5 * con_c, -con_b, push_x, push_y,
-         -0.5 * (off_x * push_x + off_y * push_y)],
-        8,
-    )
-    coef = jnp.concatenate(parts_of(coef, 3), axis=0).astype(bf16)
     colour = parts_of(slot[8:16], 3)
     colour = jnp.concatenate(
         [colour[0], colour[1], colour[2], colour[0], colour[1], colour[0]], axis=0
     ).astype(bf16)
-    expo[...] = dot(basis_cols, coef)
     gain[...] = dot(cot_cols, colour)
 
     groups = range(SLOTS // GROUP)
+    line_x = lax.broadcasted_iota(jnp.int32, (16, GROUP), 0).astype(f32) - 7.5
 
     def blocks(group, step):
         step((slice(None), slice(GROUP * group, GROUP * (group + 1))))
@@ -335,9 +321,17 @@
 
     for g in groups:
         def opaque(at):
-            shade = op_live[:, at[1]] * jnp.exp(expo[at])
-            alpha[at] = shade
-            split_to(jnp.log(1.0 - shade), keep_a, keep_b, at)
+            cols = at[1]
+            gap_x = line_x - off_x[:, cols]
+            square = -0.5 * con_a[:, cols] * gap_x * gap_x
+            cross = con_b[:, cols] * gap_x
+            for y in range(16):
+                gap_y = (y - 7.5) - off_y[:, cols]
+                expo = square + (-0.5 * con_c[:, cols] * gap_y * gap_y - cross * gap_y)
+                shade = op_live[:, cols] * jnp.exp(expo)
+                line = (slice(16 * y, 16 * (y + 1)), cols)
+                alpha[line] = shade
+                split_to(jnp.log(1.0 - shade), keep_a, keep_b, line)
 
         blocks(g, opaque)
 
@@ -356,13 +350,22 @@
         if g + 1 < len(groups):
             carried = edge_of(inside, keep_a, keep_b, GROUP * (g + 1) - 1)
 
+    tints = [[], [], []]
     for g in groups:
         def weigh(at):
-            weight = alpha[at] * jnp.exp(before[at])
-            split_to(weight, weight_a, weight_b, at)
-            weighted = gain[at] * weight
-            wgain[at] = weighted
-            split_to(weighted, keep_a, keep_b, at)
+            sums = [None] * 3
+            for y in range(16):
+                line = (slice(16 * y, 16 * (y + 1)), at[1])
+                weight = alpha[line] * jnp.exp(before[line])
+                for channel in range(3):
+                    column = cot_wide[channel, line[0], :]
+                    term = jnp.concatenate([column, column], axis=1) * weight
+                    sums[channel] = term if y == 0 else sums[channel] + term
+                weighted = gain[line] * weight
+                wgain[line] = weighted
+                split_to(weighted, keep_a, keep_b, line)
+            for channel in range(3):
+                tints[channel].append(jnp.sum(sums[channel], axis=0, keepdims=True))
 
         blocks(g, weigh)
 
@@ -376,18 +379,29 @@
         if g:
             carried = edge_of(inside, keep_a, keep_b, GROUP * g)
 
+    moments = [[] for _ in range(6)]
     for g in groups:
         def drop(at):
-            shade = alpha[at]
-            split_to(wgain[at] - behind[at] * (shade / (1.0 - shade)), drop_a, drop_b, at)
+            plain = lifted = squared = None
+            for y in range(16):
+                line = (slice(16 * y, 16 * (y + 1)), at[1])
+                shade = alpha[line]
+                value = wgain[line] - behind[line] * (shade / (1.0 - shade))
+                place = y - 7.5
+                raised = place * value
+                plain = value if y == 0 else plain + value
+                lifted = raised if y == 0 else lifted + raised
+                squared = place * raised if y == 0 else squared + place * raised
+            pushed = line_x * plain
+            for i, term in enumerate(
+                (line_x * pushed, squared, line_x * lifted, pushed, lifted, plain)
+            ):
+                moments[i].append(jnp.sum(term, axis=0, keepdims=True))
 
         blocks(g, drop)
 
-    tint = dot(cot_rows, weight_a[...]) + dot(cot_rows, weight_b[...])
-    tint = tint[0:8] + tint[8:16]
-    moment = dot(basis_rows, drop_a[...]) + dot(basis_rows, drop_b[...])
-    m_xx, m_yy, m_xy = moment[0:1], moment[1:2], moment[2:3]
-    m_x, m_y, m_one = moment[3:4], moment[4:5], moment[5:6]
+    tint = stack_rows([jnp.concatenate(parts, axis=1) for parts in tints], 8)
+    m_xx, m_yy, m_xy, m_x, m_y, m_one = (jnp.concatenate(parts, axis=1) for parts in moments)
     m_du = m_x - off_x * m_one
     m_dv = m_y - off_y * m_one
     slot_grad = stack_rows(
@@ -510,14 +524,10 @@
             pltpu.VMEM((3 * N_TILE, SLOTS), bf16),
             pltpu.VMEM(plane, f32),
             pltpu.VMEM(plane, f32),
-            pltpu.VMEM(plane, f32),
             pltpu.VMEM(plane, bf16),
             pltpu.VMEM(plane, bf16),
             pltpu.VMEM(plane, f32),
-            pltpu.VMEM(plane, bf16),
-            pltpu.VMEM(plane, bf16),
-            pltpu.VMEM(plane, bf16),
-            pltpu.VMEM(plane, bf16),
+            pltpu.VMEM((3, PIX, 128), f32),
             pltpu.VMEM(plane, f32),
             pltpu.VMEM(plane, f32),
             pltpu.VMEM((128, 128), jnp.int32),

time: 46.1 us -> 46.3 us (level)
  no operation moved by 1% of the time
where the time goes in v4:
time: 46.3 us; the launch traced here: 46.1 us
  Pallas kernels  44.8 us (97%)
  between operations  1.29 us (3%)
    pallas_call x1, Pallas kernels, body(): pl.pallas_call(splat_kernel, out_shape=[pltpu.VMEM((N_CAM, 10, 1, OWN), f...  43.5 us
    pallas_call x1, Pallas kernels, body(): pl.pallas_call(update_kernel, out_shape=(leaf, leaf, leaf, leaf), in_spec...  1.37 us

profile of v4, /device:TPU:1, one launch (start us, length us, event | category | flops | bytes accessed | tf_op | source)
XLA Modules:
  0.0 46.1 jit_solution(15371686243279988398)
XLA Ops:
  1.3 43.5 %splat.1 = (f32[4,10,1,512]{3,2,1,0:T(1,128)S(1)}, f32[59,512]{1,0:T(8,128)S(1)}, f32[59,512]{1,0:T(8,128)S(1)}, f32[59,512]{1,0:T(8,128)S(1)}) custom-call(f32[59,512]{1,0:T(8,128)} %gauss_any.1, f32[1,4]{1,0:T(1,128)} %camera_any.1, s32[1,1024]{1,0:T(1,128)} %req_any.1, s32[1,1024]{1,0:T(1,128)} %bitcast.2, s32[1,1]{1,0:T(1,128)S(6)} %copy.12.length_any, ...), custom_call_target="tpu_custom_call" | custom-call | tf_op jit(solution)/shard_map/splat/pallas_call | solution.py:506
  44.7 1.4 %update.1 = (f32[59,512]{1,0:T(8,128)}, f32[59,512]{1,0:T(8,128)}, f32[59,512]{1,0:T(8,128)}, f32[59,512]{1,0:T(8,128)}) custom-call(f32[59,512]{1,0:T(8,128)S(1)} %get-tuple-element.8.gauss_ref, f32[59,512]{1,0:T(8,128)S(1)} %get-tuple-element.9.one_ref, f32[59,512]{1,0:T(8,128)S(1)} %get-tuple-element.10.two_ref, ...), custom_call_target="tpu_custom_call" | custom-call | tf_op jit(solution)/shard_map/update/pallas_call | solution.py:547
